TPU v7x, 256 devices: a whole 4x4x8 slice. The times are simulated.
256 devices in a mesh: leaf: 64 (over y, z, core), rhs: 4 (over x).
Axes of the slice: x: 4, y: 4, z: 8, core: 2. Of those that a mesh axis runs over, the one named last changes fastest.
Arguments:
- leaf_right: float32 [2048, 256, 128], P('leaf', 'rhs'), may hold values from -6 to 6
- upper_right: float32 [128, 256, 128], P('leaf', 'rhs'), may hold values from -6 to 6
- leaf_inverse: bfloat16 [2048, 128, 128], P(('leaf', 'rhs')), as said below
- upper_inverse: bfloat16 [128, 128, 128], P('leaf'), as said below
- update_blocks: bfloat16 [16384, 128, 128], P('leaf'), may hold values from -0.046875 to 0.046875
- block_target: int32 [16384, 1], P('leaf'), may hold values from 0 to 127; in each aligned block of 256 rows (0 to 255, 256 to 511, ...) at most 4 rows name the same one
- upper_place: int32 [128], replicated, may hold values from 0 to 127, each once
Outputs:
- leaf_solution: float32 [2048, 256, 128], P('leaf', 'rhs')
- upper_solution: float32 [128, 256, 128], P('leaf', 'rhs')
Inputs may be any that keep to these rules, and one draw needn't show every extreme that they name: `leaf_inverse`: lower triangular blocks, diagonal entries between 0.6 and 1.4. `upper_inverse`: lower triangular blocks, diagonal entries between 0.6 and 1.4. `block_target`: among the 256 blocks of one device no upper supernode is named more than 4 times, a bound that some block reaches. `upper_place`: each row of the upper arrays holds exactly one upper supernode.
All inputs are finite; a program needn't handle non-finite values.
Results may differ from a plain program's by a relative error of at most 0.0049.
Values may be sent and summed in bfloat16 or wider, within the bound.
A program may use at most 64 MiB of HBM per device.

v0:
```python
import jax
import jax.numpy as jnp
from jax import lax
from jax.sharding import PartitionSpec as P


def on_device(
    leaf_right, upper_right, leaf_inverse, upper_inverse, update_blocks, block_target, upper_place
):
    inverse_mine = lax.all_gather(leaf_inverse, "rhs", axis=0, tiled=True)
    leaf_rounded = leaf_right.astype(jnp.bfloat16)
    leaf_forward = jnp.einsum(
        "ncw,nvw->ncv", leaf_rounded, inverse_mine, preferred_element_type=jnp.float32
    )
    leaf_half = leaf_forward.astype(jnp.bfloat16)
    leaf_count, columns, width = leaf_forward.shape
    block_count = update_blocks.shape[0]
    per_leaf = block_count // leaf_count
    grouped = update_blocks.reshape(leaf_count, per_leaf, width, width)
    updates = jnp.einsum("ncw,nbvw->nbcv", leaf_half, grouped, preferred_element_type=jnp.float32)
    updates = updates.reshape(block_count, columns, width)
    upper_total = upper_place.shape[0]
    table = jnp.arange(upper_total, dtype=jnp.int32)
    position = jnp.sum(jnp.where(block_target == table[None, :], upper_place[None, :], 0), axis=1)
    upper_rows = upper_right.shape[0]
    local_index = position
    inside = (local_index >= 0) & (local_index < upper_rows * lax.axis_size("leaf"))
    local_index = jnp.where(inside, local_index, upper_rows * lax.axis_size("leaf"))
    upper_sums = lax.psum_scatter(
        jax.ops.segment_sum(updates, local_index, num_segments=upper_rows * lax.axis_size("leaf")),
        "leaf",
        scatter_dimension=0,
        tiled=True,
    )
    upper_rounded = (upper_right - upper_sums).astype(jnp.bfloat16)
    upper_half = jnp.einsum(
        "pcw,pvw->pcv", upper_rounded, upper_inverse, preferred_element_type=jnp.float32
    ).astype(jnp.bfloat16)
    upper_solution = jnp.einsum(
        "pcw,pwv->pcv", upper_half, upper_inverse, preferred_element_type=jnp.float32
    )
    upper_sent = upper_solution.astype(jnp.bfloat16)
    solved_table = lax.all_gather(upper_sent, "leaf", axis=0, tiled=True)
    chosen = jnp.take(solved_table, position, axis=0)
    corrections = jnp.einsum(
        "kcv,kvw->kcw", chosen, update_blocks, preferred_element_type=jnp.float32
    )
    corrections = corrections.reshape(leaf_count, per_leaf, columns, width).sum(axis=1)
    leaf_back = (leaf_forward - corrections).astype(jnp.bfloat16)
    leaf_solution = jnp.einsum(
        "ncw,nwv->ncv", leaf_back, inverse_mine, preferred_element_type=jnp.float32
    )
    return (leaf_solution, upper_solution)


def solution(mesh):
    return jax.shard_map(
        on_device,
        mesh=mesh,
        in_specs=(
            P("leaf", "rhs", None),
            P("leaf", "rhs", None),
            P(("leaf", "rhs"), None, None),
            P("leaf", None, None),
            P("leaf", None, None),
            P("leaf", None),
            P(),
        ),
        out_specs=(P("leaf", "rhs", None), P("leaf", "rhs", None)),
        check_vma=False,
    )
```

profile of v0, /device:TPU:1, one launch (start us, length us, event | category | flops | bytes accessed | tf_op | source)
XLA Modules:
  0.0 338.4 jit_solution(17346281940933567968)
XLA Ops:
  7.2 0.0 copy-start
  7.2 0.0 all-gather.3.cloned.1.call-start
  7.2 0.7 all-gather.3.cloned.1.call-update
  7.9 0.0 reduce-scatter.2.cloned.1.call-start
  8.0 0.9 select_reduce_fusion
  8.8 30.4 %all-gather.3.cloned.1.call-done = bf16[32,128,128]{2,1,0:T(8,128)(2,1)} async-done(((bf16[8,128,128]{2,1,0:T(8,128)(2,1)}), bf16[32,128,128]{2,1,0:T(8,128)(2,1)}) %all-gather.3.cloned.1.call-update) | async-done | bytes 1048592 | tf_op jit(solution)/shard_map/all_gather | solution.py:10
  39.2 2.3 fusion.11
  41.6 9.6 %fusion.8 = f32[32,64,8,128]{3,1,2,0:T(8,128)} fusion(bf16[32,8,128,128]{3,2,1,0:T(8,128)(2,1)} %bitcast.22, f32[32,64,128]{2,1,0:T(8,128)S(1)} %fusion.11), kind=kOutput, calls=%fused_computation.11 | convolution fusion | flops 537133056 | bytes 17825792 | tf_op jit(solution)/shard_map/ncw,nbvw->nbcv/dot_general | solution.py:20
  51.2 2.5 broadcast_in_dim.33
  53.7 39.9 %scatter_fusion = f32[128,64,128]{2,1,0:T(8,128)} fusion(f32[128,64,128]{2,1,0:T(8,128)} %broadcast_in_dim.33, s32[256]{0:T(256)S(1)} %bitcast.23, f32[256,64,128]{2,1,0:T(8,128)} %bitcast.21), kind=kCustom, calls=%fused_computation.1 | custom fusion | flops 2097152 | bytes 25166848 | tf_op jit(solution)/shard_map/scatter-add | solution.py:30
  93.6 0.0 copy-start.2
  93.6 0.0 reduce-scatter.2.cloned.1.call-update
  93.6 0.0 all-gather.5.cloned.1.call-start
  93.7 140.1 %reduce-scatter.2.cloned.1.call-done = f32[2,64,128]{2,1,0:T(8,128)} async-done(((f32[128,64,128]{2,1,0:T(8,128)}), f32[2,64,128]{2,1,0:T(8,128)}) %reduce-scatter.2.cloned.1.call-update) | async-done | bytes 65552 | tf_op jit(solution)/shard_map/reduce_scatter | solution.py:29
  233.8 0.0 copy-done
  233.8 0.0 copy-done.2
  233.8 1.7 fusion.14
  235.5 0.0 all-gather.5.cloned.1.call-update
  235.6 83.0 %all-gather.5.cloned.1.call-done = bf16[128,64,128]{2,1,0:T(8,128)(2,1)} async-done(((bf16[2,64,128]{2,1,0:T(8,128)(2,1)}), bf16[128,64,128]{2,1,0:T(8,128)(2,1)}) %all-gather.5.cloned.1.call-update) | async-done | bytes 2097168 | tf_op jit(solution)/shard_map/all_gather | solution.py:43
  318.6 4.6 %gather_fusion = bf16[256,64,128]{2,1,0:T(8,128)(2,1)} fusion(bf16[128,64,128]{2,1,0:T(8,128)(2,1)} %all-gather.5.cloned.1.call-done, s32[1024]{0:T(1024)S(1)} %pad_clamp_fusion), kind=kCustom, calls=%fused_computation | custom fusion | bytes 8389632 | tf_op jit(solution)/shard_map/jit(_take)/gather | solution.py:44
  323.3 0.0 copy-start.1
  323.3 7.2 %bitcast_reduce_fusion = f32[32,64,128]{2,1,0:T(8,128)S(1)} fusion(bf16[256,128,128]{2,1,0:T(8,128)(2,1)} %param.11, bf16[256,64,128]{2,1,0:T(8,128)(2,1)} %gather_fusion, pred[256]{0:T(512)(128)(4,1)S(1)} %compare_and_fusion), kind=kOutput, calls=%fused_computation.2 | convolution fusion | flops 540803072 | bytes 13631744 | tf_op jit(solution)/shard_map/kcv,kvw->kcw/dot_general | solution.py:45
  330.4 0.0 copy-done.1
  330.4 1.4 fusion.7
  (3 shorter events, 0.0 us)
Async XLA Ops:
  7.2 226.6 %copy-start = (bf16[2,128,128]{2,1,0:T(8,128)(2,1)S(1)}, bf16[2,128,128]{2,1,0:T(8,128)(2,1)}, u32[]{:S(2)}) copy-start(bf16[2,128,128]{2,1,0:T(8,128)(2,1)} %param.10) | copy-start | bytes 196612
  7.2 32.1 %all-gather.3.cloned.1.call-start = ((), (), s32[]{:S(2)}) async-start(), calls=%async_computation.1 | async-start | bytes 1310720 | tf_op jit(solution)/shard_map/all_gather | solution.py:10
  7.9 225.9 %reduce-scatter.2.cloned.1.call-start = ((), (), s32[]{:S(2)}) async-start(), calls=%async_computation.2 | async-start | bytes 4259840 | tf_op jit(solution)/shard_map/reduce_scatter | solution.py:29
  93.6 140.2 %copy-start.2 = (f32[2,64,128]{2,1,0:T(8,128)S(1)}, f32[2,64,128]{2,1,0:T(8,128)}, u32[]{:S(2)}) copy-start(f32[2,64,128]{2,1,0:T(8,128)} %param.8) | copy-start | bytes 196612
  93.6 225.0 %all-gather.5.cloned.1.call-start = ((), (), s32[]{:S(2)}) async-start(), calls=%async_computation.3 | async-start | bytes 2129920 | tf_op jit(solution)/shard_map/all_gather | solution.py:43
  323.3 7.2 %copy-start.1 = (bf16[32,128,128]{2,1,0:T(8,128)(2,1)S(1)}, bf16[32,128,128]{2,1,0:T(8,128)(2,1)}, u32[]{:S(2)}) copy-start(bf16[32,128,128]{2,1,0:T(8,128)(2,1)} %all-gather.3.cloned.1.call-done) | copy-start | bytes 3145732
Sparse Core Ops, SparseCore 0:
  9.8 29.3 all-gather.2
  93.8 139.9 reduce-scatter.1
  237.5 81.0 all-gather.4
where the time goes:
time: 339 us; the launch traced here: 338 us
  waiting for transfers between devices  254 us (75%)
  other arithmetic  40.8 us (12%)
  matrix products  22.3 us (7%)
  between operations  13.8 us (4%)
  local copies, waits for them, and re-layouts  7.11 us (2%)
    reduce_scatter x1, waiting for transfers between devices, on_device(): lax.psum_scatter(jax.ops.segment_sum(updates, local_index, num_segments=u...  140 us
    all_gather x1, waiting for transfers between devices, on_device(): solved_table = lax.all_gather(upper_sent, 'leaf', axis=0, tiled=True)  83 us
    scatter-add x1, other arithmetic, on_device(): jax.ops.segment_sum(updates, local_index, num_segments=upper_rows * lax.a...  39.9 us
    all_gather x1, waiting for transfers between devices, on_device(): inverse_mine = lax.all_gather(leaf_inverse, 'rhs', axis=0, tiled=True)  30.4 us
    dot_general x1, matrix products, on_device(): jnp.einsum('ncw,nbvw->nbcv', leaf_half, grouped, preferred_element_type=j...  9.63 us
    dot_general x1, matrix products, on_device(): jnp.einsum('kcv,kvw->kcw', chosen, update_blocks, preferred_element_type=...  7.16 us
  transfers between devices with their start and end apart: 3, of which 3 were waited for; matrix products, arithmetic and copies ran while one was open for 0% of the time, Pallas kernels for 0%

commit v1 on v0

--- a/solution.py
+++ b/solution.py
@@ -7,7 +7,29 @@
 def on_device(
     leaf_right, upper_right, leaf_inverse, upper_inverse, update_blocks, block_target, upper_place
 ):
-    inverse_mine = lax.all_gather(leaf_inverse, "rhs", axis=0, tiled=True)
+    val2, everything, lower = (lax.axis_size("rhs"), lax.axis_index("rhs"), leaf_inverse.shape[0])
+    pile = [(h, (h + 1) % val2) for h in range(val2)]
+    samples = [(h, (h - 1) % val2) for h in range(val2)]
+    inverse_mine = jnp.zeros(
+        (*leaf_inverse.shape[:0], val2 * lower, *leaf_inverse.shape[1:]), leaf_inverse.dtype
+    )
+    inverse_mine = lax.dynamic_update_slice_in_dim(
+        inverse_mine, leaf_inverse, everything * lower, axis=0
+    )
+    newest = raw_out = leaf_inverse
+    placed = val2 // 2
+    t = 1
+    while t < placed + 1:
+        newest = lax.ppermute(newest, "rhs", pile)
+        inverse_mine = lax.dynamic_update_slice_in_dim(
+            inverse_mine, newest, (everything - t) % val2 * lower, axis=0
+        )
+        if t < val2 - placed:
+            raw_out = lax.ppermute(raw_out, "rhs", samples)
+            inverse_mine = lax.dynamic_update_slice_in_dim(
+                inverse_mine, raw_out, (everything + t) % val2 * lower, axis=0
+            )
+        t += 1
     leaf_rounded = leaf_right.astype(jnp.bfloat16)
     leaf_forward = jnp.einsum(
         "ncw,nvw->ncv", leaf_rounded, inverse_mine, preferred_element_type=jnp.float32

time: 339 us -> 325 us (0.959)
  waiting for transfers between devices: 254 us -> 234 us
  starting transfers between devices: 0.12 us -> 5.41 us
    all_gather x1 -> x0, waiting for transfers between devices: 30.4 us -> none  [on_device(): inverse_mine = lax.all_gather(leaf_inverse, 'rhs', axis=0, tiled=True)]
    ppermute x0 -> x3, waiting for transfers between devices: none -> 6.91 us  [the longest x2 6.91 us: on_device(): newest = lax.ppermute(newest, 'rhs', pile)]
    ppermute x0 -> x3, starting transfers between devices: none -> 5.33 us  [the longest x2 3.97 us: on_device(): newest = lax.ppermute(newest, 'rhs', pile)]
    reduce_scatter x1, waiting for transfers between devices: 140 us -> 144 us  [on_device(): lax.psum_scatter(jax.ops.segment_sum(updates, local_index, num_segments=u...]
  transfers between devices with their start and end apart: 3 -> 5, of which waited for: 3 -> 4; matrix products, arithmetic and copies ran while one was open for 0% -> 1% of each run, Pallas kernels for 0% -> 0%
where the time goes in v1:
time: 325 us; the launch traced here: 324 us
  waiting for transfers between devices  234 us (72%)
  other arithmetic  40.3 us (12%)
  matrix products  21.9 us (7%)
  between operations  14.2 us (4%)
  local copies, waits for them, and re-layouts  8.44 us (3%)
  starting transfers between devices  5.41 us (2%)
    reduce_scatter x1, waiting for transfers between devices, on_device(): lax.psum_scatter(jax.ops.segment_sum(updates, local_index, num_segments=u...  144 us
    all_gather x1, waiting for transfers between devices, on_device(): solved_table = lax.all_gather(upper_sent, 'leaf', axis=0, tiled=True)  83.1 us
    scatter-add x1, other arithmetic, on_device(): jax.ops.segment_sum(updates, local_index, num_segments=upper_rows * lax.a...  39.4 us
    dot_general x1, matrix products, on_device(): jnp.einsum('ncw,nbvw->nbcv', leaf_half, grouped, preferred_element_type=j...  9.64 us
    dot_general x1, matrix products, on_device(): jnp.einsum('kcv,kvw->kcw', chosen, update_blocks, preferred_element_type=...  7.1 us
    ppermute x2, waiting for transfers between devices, on_device(): newest = lax.ppermute(newest, 'rhs', pile)  6.91 us
  transfers between devices with their start and end apart: 5, of which 4 were waited for; matrix products, arithmetic and copies ran while one was open for 1% of the time, Pallas kernels for 0%

profile of v1, /device:TPU:1, one launch (start us, length us, event | category | flops | bytes accessed | tf_op | source)
XLA Modules:
  0.0 324.1 jit_solution(6959597418613802002)
XLA Ops:
  7.2 0.0 copy-start
  7.2 0.0 reduce-scatter.2.cloned.1.call-start
  7.2 2.1 collective-permute-start
  9.3 1.4 collective-permute-start.1
  10.7 0.9 select_reduce_fusion
  11.6 3.0 collective-permute-done
  14.6 1.9 collective-permute-start.2
  16.4 0.2 broadcast_in_dim.33
  16.7 1.0 constant_dynamic-update-slice_fusion.3
  17.8 0.0 collective-permute-done.1
  17.8 3.9 %collective-permute-done.2 = bf16[8,128,128]{2,1,0:T(8,128)(2,1)S(1)} collective-permute-done((bf16[8,128,128]{2,1,0:T(8,128)(2,1)S(1)}, bf16[8,128,128]{2,1,0:T(8,128)(2,1)S(1)}, u32[]{:S(2)}, u32[]{:S(2)}) %collective-permute-start.2) | collective-permute-done | bytes 262176 | tf_op jit(solution)/shard_map/ppermute | solution.py:23
  21.8 2.0 convolution_bitcast_fusion
  23.8 9.6 %fusion.8 = f32[32,64,8,128]{3,1,2,0:T(8,128)} fusion(bf16[32,8,128,128]{3,2,1,0:T(8,128)(2,1)} %bitcast.24, f32[32,64,128]{2,1,0:T(8,128)S(1)} %convolution_bitcast_fusion), kind=kOutput, calls=%fused_computation.12 | convolution fusion | flops 537133056 | bytes 17825792 | tf_op jit(solution)/shard_map/ncw,nbvw->nbcv/dot_general | solution.py:42
  33.5 2.5 broadcast_in_dim.37
  35.9 39.4 %scatter_fusion = f32[128,64,128]{2,1,0:T(8,128)} fusion(f32[128,64,128]{2,1,0:T(8,128)} %broadcast_in_dim.37, s32[256]{0:T(256)S(1)} %bitcast.25, f32[256,64,128]{2,1,0:T(8,128)} %bitcast.23), kind=kCustom, calls=%fused_computation.1 | custom fusion | flops 2097152 | bytes 25166848 | tf_op jit(solution)/shard_map/scatter-add | solution.py:52
  75.4 0.0 copy-start.1
  75.4 0.0 reduce-scatter.2.cloned.1.call-update
  75.4 0.0 all-gather.2.cloned.1.call-start
  75.4 143.8 %reduce-scatter.2.cloned.1.call-done = f32[2,64,128]{2,1,0:T(8,128)} async-done(((f32[128,64,128]{2,1,0:T(8,128)}), f32[2,64,128]{2,1,0:T(8,128)}) %reduce-scatter.2.cloned.1.call-update) | async-done | bytes 65552 | tf_op jit(solution)/shard_map/reduce_scatter | solution.py:51
  219.2 0.0 copy-done
  219.2 0.0 copy-done.1
  219.2 1.7 fusion.13
  221.0 0.0 all-gather.2.cloned.1.call-update
  221.0 83.1 %all-gather.2.cloned.1.call-done = bf16[128,64,128]{2,1,0:T(8,128)(2,1)} async-done(((bf16[2,64,128]{2,1,0:T(8,128)(2,1)}), bf16[128,64,128]{2,1,0:T(8,128)(2,1)}) %all-gather.2.cloned.1.call-update) | async-done | bytes 2097168 | tf_op jit(solution)/shard_map/all_gather | solution.py:65
  304.1 4.6 %gather_fusion = bf16[256,64,128]{2,1,0:T(8,128)(2,1)} fusion(bf16[128,64,128]{2,1,0:T(8,128)(2,1)} %all-gather.2.cloned.1.call-done, s32[1024]{0:T(1024)S(1)} %pad_clamp_fusion), kind=kCustom, calls=%fused_computation | custom fusion | bytes 8389632 | tf_op jit(solution)/shard_map/jit(_take)/gather | solution.py:66
  308.7 7.1 %bitcast_reduce_fusion = f32[32,64,128]{2,1,0:T(8,128)S(1)} fusion(bf16[256,128,128]{2,1,0:T(8,128)(2,1)} %param.11, bf16[256,64,128]{2,1,0:T(8,128)(2,1)} %gather_fusion, pred[256]{0:T(512)(128)(4,1)S(1)} %compare_and_fusion), kind=kOutput, calls=%fused_computation.2 | convolution fusion | flops 540803072 | bytes 13631744 | tf_op jit(solution)/shard_map/kcv,kvw->kcw/dot_general | solution.py:67
  315.8 1.4 fusion.7
  (6 shorter events, 0.1 us)
Async XLA Ops:
  7.2 212.1 %copy-start = (bf16[2,128,128]{2,1,0:T(8,128)(2,1)S(1)}, bf16[2,128,128]{2,1,0:T(8,128)(2,1)}, u32[]{:S(2)}) copy-start(bf16[2,128,128]{2,1,0:T(8,128)(2,1)} %param.10) | copy-start | bytes 196612
  7.2 212.1 %reduce-scatter.2.cloned.1.call-start = ((), (), s32[]{:S(2)}) async-start(), calls=%async_computation.1 | async-start | bytes 4259840 | tf_op jit(solution)/shard_map/reduce_scatter | solution.py:51
  7.2 7.4 %collective-permute-start = (bf16[8,128,128]{2,1,0:T(8,128)(2,1)}, bf16[8,128,128]{2,1,0:T(8,128)(2,1)S(1)}, u32[]{:S(2)}, u32[]{:S(2)}) collective-permute-start(bf16[8,128,128]{2,1,0:T(8,128)(2,1)} %param.9), channel_id=1, source_target_pairs={{0,1},{1,2},{2,3},{3,0},{4,5},{5,6},{6,7},{7,4},{8,9},{9,10},{10,1... | collective-permute-start | bytes 786440 | tf_op jit(solution)/shard_map/ppermute | solution.py:23
  9.3 8.4 %collective-permute-start.1 = (bf16[8,128,128]{2,1,0:T(8,128)(2,1)}, bf16[8,128,128]{2,1,0:T(8,128)(2,1)S(1)}, u32[]{:S(2)}, u32[]{:S(2)}) collective-permute-start(bf16[8,128,128]{2,1,0:T(8,128)(2,1)} %param.9), channel_id=1, source_target_pairs={{0,3},{1,0},{2,1},{3,2},{4,7},{5,4},{6,5},{7,6},{8,11},{9,8},{10,9... | collective-permute-start | bytes 786440 | tf_op jit(solution)/shard_map/ppermute | solution.py:28
  14.6 7.2 %collective-permute-start.2 = (bf16[8,128,128]{2,1,0:T(8,128)(2,1)S(1)}, bf16[8,128,128]{2,1,0:T(8,128)(2,1)S(1)}, u32[]{:S(2)}, u32[]{:S(2)}) collective-permute-start(bf16[8,128,128]{2,1,0:T(8,128)(2,1)S(1)} %collective-permute-done), channel_id=1, source_target_pairs={{0,1},{1,2},{2,3},{3,0},{4,5},{5,6},{6,7},{7,4},{8,9},{9,10},{10,1... | collective-permute-start | bytes 786440 | tf_op jit(solution)/shard_map/ppermute | solution.py:23
  75.4 143.9 %copy-start.1 = (f32[2,64,128]{2,1,0:T(8,128)S(1)}, f32[2,64,128]{2,1,0:T(8,128)}, u32[]{:S(2)}) copy-start(f32[2,64,128]{2,1,0:T(8,128)} %param.8) | copy-start | bytes 196612
  75.4 228.7 %all-gather.2.cloned.1.call-start = ((), (), s32[]{:S(2)}) async-start(), calls=%async_computation.2 | async-start | bytes 2129920 | tf_op jit(solution)/shard_map/all_gather | solution.py:65
Sparse Core Ops, SparseCore 0:
  75.5 143.6 reduce-scatter.1
  223.0 81.0 all-gather.1
